TPU v7x, 512 devices: a whole 4x4x16 slice. The times are simulated.
512 devices in a mesh: gx: 8 (over x, core), gz: 64 (over z, y).
Axes of the slice: x: 4, y: 4, z: 16, core: 2. Of those that a mesh axis runs over, the one named last changes fastest.
Arguments:
- adjoint: float32 [4, 32, 512, 768], P(None, 'gx', 'gz'), may hold values from -6 to 6
- mean_velocity: float32 [512], P('gz'), may hold values from 0.2 to 1.5
- mean_shear: float32 [512], P('gz'), may hold values from -1 to 3
- viscous_inverse: float32 [512, 512], replicated
- sensor_rows: float32 [8, 64, 64, 8, 128], P('gx', 'gz'), may hold values from -6 to 6
- sensor_cells: int32 [8, 64, 64, 8], P('gx', 'gz'), may hold values from 0 to 47
- sensor_counts: int32 [8, 64, 64], P('gx', 'gz'), may hold values from 0 to 8, as said below
Outputs:
- updated: float32 [4, 32, 512, 768], P(None, 'gx', 'gz')
Inputs may be any that keep to these rules, and one draw needn't show every extreme that they name: `sensor_counts`: slots at or beyond the count are ignored. In every slab some owner receives 8 rows from every device. `sensor_cells`: entries of slots that are not used carry no meaning.
All inputs are finite; a program needn't handle non-finite values.
Results may differ from a plain program's by a relative error of at most 0.00007.
Values sent between devices are 32-bit elements; how exact they have to be, the bound alone decides.
A program may use at most 64 MiB of HBM per device.

v0:
```python
import functools

import jax
import jax.numpy as jnp
from jax import lax
from jax.experimental import pallas as pl
from jax.experimental.pallas import tpu as pltpu
from jax.sharding import PartitionSpec as P

MESH = pl.DeviceIdType.MESH
BF16 = jnp.bfloat16
F32 = jnp.float32

F, XL, NZ, NY = 4, 4, 768, 512
LEV = 8
NGX, NGZ, GY, GZ = 8, 64, 4, 16
WIN = NZ // GZ
ZL = 12
CAP = 8
KW = 32
ROWS = 12


def iota(shape, dim):
    return lax.broadcasted_iota(jnp.int32, shape, dim)


def split(x):
    hi = x.astype(BF16)
    return hi, (x - hi.astype(F32)).astype(BF16)


def dot(a, b):
    return jnp.dot(a, b, preferred_element_type=F32)


def pack(e, w):
    at = WIN * w
    first = jnp.concatenate(
        [e[0][:, at : at + 48], e[1][:, at : at + 48], e[2][:, at : at + 32]], axis=1
    )
    second = jnp.concatenate([e[2][:, at + 32 : at + 48], e[3][:, at : at + 48]], axis=1)
    return first, jnp.concatenate([second[0:4], second[4:8]], axis=1)


def kernel(
    adj_hbm, vel_ref, shear_ref, m_hbm, rows_hbm, cells_hbm, counts_hbm,
    out_ref,
    adj, halo, m_f32, mh, ml, cells, counts, wsend, wrecv, fsend, frecv, bsend, brecv, xsend, xrecv,
    local_sem, halo_send, halo_recv, w_send, w_recv, f_send, f_recv, b_send, b_recv, x_send, x_recv,
):
    gx = lax.axis_index("gx")
    me = lax.axis_index("gz")
    z = me // GY
    y = lax.rem(me, GY)

    def remote(src, dst, ss, rs, ix, iz):
        return pltpu.make_async_remote_copy(
            src_ref=src, dst_ref=dst, send_sem=ss, recv_sem=rs, device_id=(ix, iz), device_id_type=MESH
        )

    barrier = pltpu.get_barrier_semaphore()
    after, before = lax.rem(gx + 1, NGX), lax.rem(gx + NGX - 1, NGX)
    for ix in (after, before):
        pl.semaphore_signal(barrier, inc=1, device_id=(ix, me), device_id_type=MESH)

    def greet(i, c):
        pl.semaphore_signal(
            barrier, inc=1, device_id=(gx, lax.rem(me + i, NGZ)), device_id_type=MESH
        )
        return c

    lax.fori_loop(1, NGZ, greet, 0)

    loads = [
        pltpu.make_async_copy(adj_hbm, adj, local_sem.at[0]),
        pltpu.make_async_copy(cells_hbm.at[0, 0], cells, local_sem.at[1]),
        pltpu.make_async_copy(counts_hbm.at[0], counts, local_sem.at[2]),
        pltpu.make_async_copy(rows_hbm.at[0, 0], wsend.at[:, pl.ds(0, CAP)], local_sem.at[3]),
        pltpu.make_async_copy(m_hbm, m_f32, local_sem.at[4]),
    ]
    for load in loads:
        load.start()

    loads[1].wait()
    loads[2].wait()
    counts_row = jnp.broadcast_to(counts[...].astype(F32), (NGZ, NGZ))
    diagonal = iota((NGZ, NGZ), 0) == iota((NGZ, NGZ), 1)
    counts_col = jnp.sum(jnp.where(diagonal, counts_row, 0.0), axis=1, keepdims=True)
    slot = iota((NGZ, CAP), 1).astype(F32)
    used_cells = jnp.where(slot < counts_col, cells[...].astype(F32), -1.0)
    loads[3].wait()
    wsend[:, CAP, :] = jnp.concatenate(
        [used_cells, jnp.zeros((NGZ, 128 - CAP), F32)], axis=1
    )

    level = iota((LEV, NZ), 0)
    velocity = jnp.zeros((LEV, NZ), F32)
    shear = jnp.zeros((LEV, NZ), F32)
    for i in range(LEV):
        velocity = jnp.where(level == i, vel_ref[i], velocity)
        shear = jnp.where(level == i, shear_ref[i], shear)

    def step_and_pack(x):
        rows = []
        for f in range(F):
            here = adj[f, x]
            up = adj[f, x + 1] if x < XL - 1 else halo[1, f]
            down = adj[f, x - 1] if x > 0 else halo[0, f]
            spanwise = pltpu.roll(here, NZ - 1, 1) + pltpu.roll(here, 1, 1) - 2.0 * here
            e = here + 0.5 * velocity * ((up - down) / 2.0) + 0.25 * spanwise
            if f == 1:
                e = e + 0.5 * shear * adj[0, x]
            rows.append(e)
        for w in range(GZ):
            first, second = pack(rows, w)
            fsend[w * GY + x, 0:8, :] = first
            fsend[w * GY + x, 8:12, :] = second

    loads[0].wait()
    step_and_pack(1)
    step_and_pack(2)

    pl.semaphore_wait(barrier, NGZ - 1 + 2)

    halos = [
        remote(adj.at[:, XL - 1], halo.at[0], halo_send.at[0], halo_recv.at[0], after, me),
        remote(adj.at[:, 0], halo.at[1], halo_send.at[1], halo_recv.at[1], before, me),
    ]
    for h in halos:
        h.start()

    def send_wall(i, c):
        d = lax.rem(me + i, NGZ)
        remote(wsend.at[d], wrecv.at[me], w_send, w_recv, gx, d).start()
        return c

    lax.fori_loop(1, NGZ, send_wall, 0)
    wrecv[me] = wsend[me]

    def send_fields(first, second):
        def body(i, c):
            for x in (first, second):
                d = lax.rem(z + i, GZ) * GY + x

                @pl.when(d != me)
                def _():
                    remote(fsend.at[d], frecv.at[me], f_send, f_recv, gx, d).start()

            return c

        lax.fori_loop(0, GZ, body, 0)

    send_fields(1, 2)
    for h in halos:
        h.wait_recv()
    step_and_pack(0)
    step_and_pack(3)
    send_fields(0, 3)
    frecv[me] = fsend[me]

    loads[4].wait()
    m_hi, m_lo = split(m_f32[...])
    mh[...] = m_hi
    ml[...] = m_lo

    others = pl.ds(0, NGZ - 1)
    pltpu.make_async_copy(wsend.at[others], wrecv.at[others], w_recv).wait()
    slots = NGZ * CAP
    got = wrecv[:, CAP, :].astype(BF16)[:, 0:CAP]
    tile = (iota((CAP, slots), 0) == lax.rem(iota((CAP, slots), 1), CAP)).astype(BF16)
    spread = dot(got, tile)
    mine = iota((NGZ, slots), 0) == iota((NGZ, slots), 1) // CAP
    cell_row = jnp.sum(jnp.where(mine, spread, 0.0), axis=0, keepdims=True)
    place = iota((64, slots), 0)
    inside = lax.rem(place, 16) < ZL
    target = jnp.where(inside, (place // 16) * ZL + lax.rem(place, 16), -2).astype(F32)
    onehot = jnp.where(target == cell_row, 1.0, 0.0).astype(BF16)
    r_hi, r_lo = split(wrecv[:, 0:CAP, :].reshape(slots, 128))
    wall = dot(onehot, r_hi) + dot(onehot, r_lo)
    xsend[...] = wall.reshape(XL, 16, 128)
    for k in range(1, GY):
        other = lax.rem(y + k, GY)
        remote(
            xsend.at[other], xrecv.at[y], x_send.at[k - 1], x_recv.at[k - 1], gx, z * GY + other
        ).start()
    xrecv[y] = xsend[y]
    for k in range(1, GY):
        pltpu.make_async_copy(xsend.at[0], xrecv.at[0], x_recv.at[k - 1]).wait()
    wall_t = jnp.transpose(xrecv[...].reshape(64, 128))
    p = iota((64, 192), 0)
    col = iota((64, 192), 1)
    forcing = jnp.zeros((KW, 192), F32)
    for f in range(F):
        there = (lax.rem(p, 16) < ZL) & (col == WIN * f + ZL * (p // 16) + lax.rem(p, 16))
        there = jnp.where(there, 1.0, 0.0).astype(BF16)
        v_hi, v_lo = split(wall_t[KW * f : KW * (f + 1)])
        forcing = forcing + dot(v_hi, there) + dot(v_lo, there)

    pltpu.make_async_copy(fsend.at[others], frecv.at[others], f_recv).wait()
    left = frecv[:, 0:8, :].reshape(NY, 128)
    tail = frecv[:, 8:12, :]
    right = jnp.concatenate([tail[:, :, 0:64], tail[:, :, 64:128]], axis=1).reshape(NY, 64)
    columns = jnp.concatenate([left, right], axis=1)
    columns = jnp.concatenate([columns[0:KW] + forcing, columns[KW:]], axis=0)
    c_hi, c_lo = split(columns)
    solved = dot(mh[...], c_hi) + dot(mh[...], c_lo) + dot(ml[...], c_hi)
    bsend[:, 0:8, :] = solved[:, 0:128].reshape(NGZ, LEV, 128)
    back = solved[:, 128:192].reshape(NGZ, LEV, 64)
    bsend[:, 8:12, :] = jnp.concatenate([back[:, 0:4, :], back[:, 4:8, :]], axis=2)

    def send_back(i, c):
        d = lax.rem(me + i, NGZ)
        remote(bsend.at[d], brecv.at[me], b_send, b_recv, gx, d).start()
        return c

    lax.fori_loop(1, NGZ, send_back, 0)
    brecv[me] = bsend[me]
    pltpu.make_async_copy(bsend.at[others], brecv.at[others], b_recv).wait()

    for x in range(XL):
        pieces = [[] for _ in range(F)]
        for w in range(GZ):
            b0 = brecv[w * GY + x, 0:8, :]
            b1 = brecv[w * GY + x, 8:12, :]
            b1 = jnp.concatenate([b1[:, 0:64], b1[:, 64:128]], axis=0)
            pieces[0].append(b0[:, 0:48])
            pieces[1].append(b0[:, 48:96])
            pieces[2].append(b0[:, 96:128])
            pieces[2].append(b1[:, 0:16])
            pieces[3].append(b1[:, 16:64])
        for f in range(F):
            out_ref[f, x] = jnp.concatenate(pieces[f], axis=1)

    for h in halos:
        h.wait_send()
    pltpu.make_async_copy(wsend.at[others], wrecv.at[others], w_send).wait()
    pltpu.make_async_copy(fsend.at[others], frecv.at[others], f_send).wait()
    pltpu.make_async_copy(bsend.at[others], brecv.at[others], b_send).wait()
    for k in range(1, GY):
        pltpu.make_async_copy(xsend.at[0], xrecv.at[0], x_send.at[k - 1]).wait()


def on_device(adjoint, velocity, shear, matrix, rows, cells, counts):
    anywhere = pl.BlockSpec(memory_space=pl.ANY)
    smem = pl.BlockSpec(memory_space=pltpu.SMEM)
    vmem = pltpu.VMEM
    dma = pltpu.SemaphoreType.DMA
    message = vmem((NGZ, ROWS, 128), F32)
    return pl.pallas_call(
        kernel,
        out_shape=jax.ShapeDtypeStruct((F, XL, LEV, NZ), F32),
        in_specs=[anywhere, smem, smem, anywhere, anywhere, anywhere, anywhere],
        out_specs=pl.BlockSpec(memory_space=pltpu.VMEM),
        scratch_shapes=[
            vmem((F, XL, LEV, NZ), F32),
            vmem((2, F, LEV, NZ), F32),
            vmem((NY, NY), F32),
            vmem((NY, NY), BF16),
            vmem((NY, NY), BF16),
            vmem((NGZ, CAP), jnp.int32),
            vmem((1, NGZ), jnp.int32),
            vmem((NGZ, CAP + 1, 128), F32),
            vmem((NGZ, CAP + 1, 128), F32),
            message, message, message, message,
            vmem((GY, 16, 128), F32),
            vmem((GY, 16, 128), F32),
            dma((5,)), dma((2,)), dma((2,)), dma, dma, dma, dma, dma, dma, dma((3,)), dma((3,)),
        ],
        compiler_params=pltpu.CompilerParams(
            collective_id=0, has_side_effects=True, vmem_limit_bytes=48 * 1024 * 1024
        ),
        cost_estimate=pl.CostEstimate(flops=310_000_000, bytes_accessed=3_000_000, transcendentals=0),
    )(adjoint, velocity, shear, matrix, rows, cells, counts)


def solution(mesh):
    in_specs = (
        P(None, "gx", "gz", None),
        P("gz"),
        P("gz"),
        P(),
        P("gx", "gz", None, None, None),
        P("gx", "gz", None, None),
        P("gx", "gz", None),
    )
    return jax.shard_map(
        on_device, mesh=mesh, in_specs=in_specs, out_specs=P(None, "gx", "gz", None), check_vma=False
    )
```

profile of v0, /device:TPU:6, one launch (start us, length us, event | category | flops | bytes accessed | tf_op | source)
XLA Modules:
  0.0 77.3 jit_solution(6918442066741611093)
XLA Ops:
  0.0 0.0 copy-start.5
  0.0 0.0 copy-start.4
  0.0 0.0 copy-start.3
  0.0 0.8 %copy.8.cells_hbm = s32[1,1,64,8]{3,2,1,0:T(8,128)S(1)} copy(s32[1,1,64,8]{2,3,1,0:T(8,128)} %param.12) | data formatting | bytes 4096 | tf_op args[5]
  0.8 0.0 copy-done.5
  0.8 0.0 copy-done.4
  0.8 0.0 copy-done.3
  0.8 0.0 copy-start
  0.8 1.2 %copy-done = f32[512,512]{1,0:T(8,128)S(1)} copy-done((f32[512,512]{1,0:T(8,128)S(1)}, f32[512,512]{1,0:T(8,128)}, u32[]{:S(2)}) %copy-start) | copy-done | bytes 1048600
  2.1 0.0 copy-start.1
  2.1 1.0 %copy-done.1 = f32[4,4,8,768]{3,2,1,0:T(8,128)S(1)} copy-done((f32[4,4,8,768]{3,2,1,0:T(8,128)S(1)}, f32[4,4,8,768]{3,2,1,0:T(8,128)}, u32[]{:S(2)}) %copy-start.1) | copy-done | bytes 393240
  3.1 0.0 copy-start.2
  3.1 0.9 %copy-done.2 = f32[1,1,64,8,128]{4,3,2,1,0:T(8,128)S(1)} copy-done((f32[1,1,64,8,128]{4,3,2,1,0:T(8,128)S(1)}, f32[1,1,64,8,128]{4,3,2,1,0:T(8,128)}, u32[]{:S(2)}) %copy-start.2) | copy-done | bytes 262168
  4.0 72.5 %shard_map.73 = f32[4,4,8,768]{3,2,1,0:T(8,128)S(1)} custom-call(f32[4,4,8,768]{3,2,1,0:T(8,128)S(1)} %copy-done.1, f32[8]{0:T(128)S(1)} %copy-done.3, f32[8]{0:T(128)S(1)} %copy-done.4, f32[512,512]{1,0:T(8,128)S(1)} %copy-done, f32[1,1,64,8,128]{4,3,2,1,0:T(8,128)S(1)} %copy-done.2, s32[1,1,64,8]{3,2,1,0:T(8,128)S(1)} %copy.8.cells_hbm, ...), custom_call_target="tpu_custom_call" | custom-call | flops 310000000 | bytes 3000000 | tf_op jit(solution)/shard_map/pallas_call | solution.py:250
  76.6 0.7 copy.10
Async XLA Ops:
  0.0 0.8 %copy-start.5 = (s32[1,1,64]{2,1,0:T(1,128)S(1)}, s32[1,1,64]{2,1,0:T(1,128)}, u32[]{:S(2)}) copy-start(s32[1,1,64]{2,1,0:T(1,128)} %counts_hbm.1) | copy-start | bytes 772
  0.0 0.8 %copy-start.4 = (f32[8]{0:T(128)S(1)}, f32[8]{0:T(128)}, u32[]{:S(2)}) copy-start(f32[8]{0:T(128)} %shear_ref.1) | copy-start | bytes 100
  0.0 0.8 %copy-start.3 = (f32[8]{0:T(128)S(1)}, f32[8]{0:T(128)}, u32[]{:S(2)}) copy-start(f32[8]{0:T(128)} %vel_ref.1) | copy-start | bytes 100
  0.8 1.2 %copy-start = (f32[512,512]{1,0:T(8,128)S(1)}, f32[512,512]{1,0:T(8,128)}, u32[]{:S(2)}) copy-start(f32[512,512]{1,0:T(8,128)} %m_hbm.1) | copy-start | bytes 3145732
  2.1 1.0 %copy-start.1 = (f32[4,4,8,768]{3,2,1,0:T(8,128)S(1)}, f32[4,4,8,768]{3,2,1,0:T(8,128)}, u32[]{:S(2)}) copy-start(f32[4,4,8,768]{3,2,1,0:T(8,128)} %adj_hbm.1) | copy-start | bytes 1179652
  3.1 0.9 %copy-start.2 = (f32[1,1,64,8,128]{4,3,2,1,0:T(8,128)S(1)}, f32[1,1,64,8,128]{4,3,2,1,0:T(8,128)}, u32[]{:S(2)}) copy-start(f32[1,1,64,8,128]{4,3,2,1,0:T(8,128)} %rows_hbm.1) | copy-start | bytes 786436
where the time goes:
time: 77.6 us; the launch traced here: 77.3 us
  Pallas kernels  72.5 us (93%)
  local copies, waits for them, and re-layouts  4.73 us (6%)
    pallas_call x1, Pallas kernels, on_device(): pl.pallas_call(kernel, out_shape=jax.ShapeDtypeStruct((F, XL, LEV, NZ), F...  72.5 us
    unnamed x14, local copies, waits for them, and re-layouts  4.73 us

commit v1 on v0

--- a/solution.py
+++ b/solution.py
@@ -18,6 +18,8 @@
 ZL = 12
 CAP = 8
 KW = 32
+NEAR = 4
+DIRECT, RIGHT, LEFT = 0, 28, 46
 ROWS = 12
 
 
@@ -46,8 +48,8 @@
 def kernel(
     adj_hbm, vel_ref, shear_ref, m_hbm, rows_hbm, cells_hbm, counts_hbm,
     out_ref,
-    adj, halo, m_f32, mh, ml, cells, counts, wsend, wrecv, fsend, frecv, bsend, brecv, xsend, xrecv,
-    local_sem, halo_send, halo_recv, w_send, w_recv, f_send, f_recv, b_send, b_recv, x_send, x_recv,
+    adj, halo, m_f32, mh, ml, cells, counts, wsend, wrecv, fsend, frecv, bsend, brecv, xsend, xrecv, dsend, drecv,
+    local_sem, halo_send, halo_recv, w_send, w_recv, f_send, f_recv, b_send, b_recv, x_send, x_recv, d_send, d_recv, known,
 ):
     gx = lax.axis_index("gx")
     me = lax.axis_index("gz")
@@ -59,18 +61,28 @@
             src_ref=src, dst_ref=dst, send_sem=ss, recv_sem=rs, device_id=(ix, iz), device_id_type=MESH
         )
 
+    def at(dz, iy):
+        return lax.rem(z + dz + GZ, GZ) * GY + iy
+
+    def signal(sem, ix, iz):
+        pl.semaphore_signal(sem, inc=1, device_id=(ix, iz), device_id_type=MESH)
+
     barrier = pltpu.get_barrier_semaphore()
     after, before = lax.rem(gx + 1, NGX), lax.rem(gx + NGX - 1, NGX)
-    for ix in (after, before):
-        pl.semaphore_signal(barrier, inc=1, device_id=(ix, me), device_id_type=MESH)
-
-    def greet(i, c):
-        pl.semaphore_signal(
-            barrier, inc=1, device_id=(gx, lax.rem(me + i, NGZ)), device_id_type=MESH
-        )
-        return c
-
-    lax.fori_loop(1, NGZ, greet, 0)
+    signal(barrier, after, me)
+    signal(barrier, before, me)
+
+    def greet_here(k, c):
+        signal(barrier, gx, at(0, lax.rem(y + k, GY)))
+        return c
+
+    def greet_near(k, c):
+        signal(barrier, gx, at(NEAR - k // GY, lax.rem(k, GY)))
+        signal(barrier, gx, at(k // GY - NEAR, lax.rem(k, GY)))
+        return c
+
+    lax.fori_loop(1, GY, greet_here, 0)
+    lax.fori_loop(0, NEAR * GY, greet_near, 0)
 
     loads = [
         pltpu.make_async_copy(adj_hbm, adj, local_sem.at[0]),
@@ -84,15 +96,11 @@
 
     loads[1].wait()
     loads[2].wait()
-    counts_row = jnp.broadcast_to(counts[...].astype(F32), (NGZ, NGZ))
-    diagonal = iota((NGZ, NGZ), 0) == iota((NGZ, NGZ), 1)
-    counts_col = jnp.sum(jnp.where(diagonal, counts_row, 0.0), axis=1, keepdims=True)
-    slot = iota((NGZ, CAP), 1).astype(F32)
-    used_cells = jnp.where(slot < counts_col, cells[...].astype(F32), -1.0)
+    used = iota((CAP, NGZ), 0) < counts[...]
+    used_cells = jnp.where(used, cells[...], -1).astype(F32)
+    used_cells = jnp.concatenate([used_cells, jnp.zeros((128 - CAP, NGZ), F32)], axis=0)
     loads[3].wait()
-    wsend[:, CAP, :] = jnp.concatenate(
-        [used_cells, jnp.zeros((NGZ, 128 - CAP), F32)], axis=1
-    )
+    wsend[:, CAP, :] = jnp.transpose(used_cells)
 
     level = iota((LEV, NZ), 0)
     velocity = jnp.zeros((LEV, NZ), F32)
@@ -121,7 +129,9 @@
     step_and_pack(1)
     step_and_pack(2)
 
-    pl.semaphore_wait(barrier, NGZ - 1 + 2)
+    pl.semaphore_wait(barrier, 2 + (GY - 1) + 2 * NEAR * GY)
+    signal(known, gx, at(NEAR, y))
+    signal(known, gx, at(-NEAR, y))
 
     halos = [
         remote(adj.at[:, XL - 1], halo.at[0], halo_send.at[0], halo_recv.at[0], after, me),
@@ -130,55 +140,110 @@
     for h in halos:
         h.start()
 
-    def send_wall(i, c):
-        d = lax.rem(me + i, NGZ)
-        remote(wsend.at[d], wrecv.at[me], w_send, w_recv, gx, d).start()
-        return c
-
-    lax.fori_loop(1, NGZ, send_wall, 0)
-    wrecv[me] = wsend[me]
-
-    def send_fields(first, second):
-        def body(i, c):
-            for x in (first, second):
-                d = lax.rem(z + i, GZ) * GY + x
-
-                @pl.when(d != me)
-                def _():
-                    remote(fsend.at[d], frecv.at[me], f_send, f_recv, gx, d).start()
-
+    def send_wall(owner_dz, dz, iy, slot):
+        owner, dest = at(owner_dz, iy), at(dz, iy)
+        remote(wsend.at[owner], wrecv.at[slot], w_send, w_recv, gx, dest).start()
+
+    def send_field(dz, x):
+        dest = at(dz, x)
+        remote(fsend.at[dest], frecv.at[me], f_send, f_recv, gx, dest).start()
+
+    def wall_here(k, c):
+        iy = lax.rem(y + k, GY)
+        send_wall(0, 0, iy, DIRECT + 3 * GY + y)
+        send_wall(4, 0, iy, RIGHT + y)
+        send_wall(-4, 0, iy, LEFT + y)
+        return c
+
+    lax.fori_loop(1, GY, wall_here, 0)
+    wrecv[DIRECT + 3 * GY + y] = wsend[me]
+    wrecv[RIGHT + y] = wsend[at(4, y)]
+    wrecv[LEFT + y] = wsend[at(-4, y)]
+
+    def wall_at(level):
+        def body(iy, c):
+            send_wall(level, level, iy, DIRECT + (3 + level) * GY + y)
+            send_wall(-level, -level, iy, DIRECT + (3 - level) * GY + y)
+            send_wall(4 + level, level, iy, RIGHT + level * GY + y)
+            send_wall(-4 - level, -level, iy, LEFT + level * GY + y)
             return c
 
-        lax.fori_loop(0, GZ, body, 0)
-
-    send_fields(1, 2)
+        lax.fori_loop(0, GY, body, 0)
+
+    for level in (1, 2, 3):
+        wall_at(level)
+    odd = lax.rem(y, 2)
+    dz8 = NEAR - 2 * NEAR * odd
+    slot8 = jnp.where(odd == 1, LEFT, RIGHT) + 4 * GY + y // 2
+
+    def wall_8(iy, c):
+        send_wall(8, dz8, iy, slot8)
+        return c
+
+    lax.fori_loop(0, GY, wall_8, 0)
+
+    def fields_at(first, last, xs):
+        def body(level, c):
+            for x in xs:
+                send_field(level, x)
+                send_field(-level, x)
+            return c
+
+        lax.fori_loop(first, last, body, 0)
+
+    def fields_here(xs):
+        for x in xs:
+
+            @pl.when(x != y)
+            def _():
+                send_field(0, x)
+
+    fields_at(1, NEAR + 1, (1, 2))
+    fields_here((1, 2))
     for h in halos:
         h.wait_recv()
     step_and_pack(0)
     step_and_pack(3)
-    send_fields(0, 3)
+    fields_at(1, NEAR + 1, (0, 3))
+    fields_here((0, 3))
     frecv[me] = fsend[me]
 
-    loads[4].wait()
-    m_hi, m_lo = split(m_f32[...])
-    mh[...] = m_hi
-    ml[...] = m_lo
-
     others = pl.ds(0, NGZ - 1)
-    pltpu.make_async_copy(wsend.at[others], wrecv.at[others], w_recv).wait()
+    got_wall = pl.ds(0, NGZ - 3)
+    pltpu.make_async_copy(wsend.at[got_wall], wrecv.at[got_wall], w_recv).wait()
     slots = NGZ * CAP
     got = wrecv[:, CAP, :].astype(BF16)[:, 0:CAP]
     tile = (iota((CAP, slots), 0) == lax.rem(iota((CAP, slots), 1), CAP)).astype(BF16)
     spread = dot(got, tile)
     mine = iota((NGZ, slots), 0) == iota((NGZ, slots), 1) // CAP
     cell_row = jnp.sum(jnp.where(mine, spread, 0.0), axis=0, keepdims=True)
-    place = iota((64, slots), 0)
-    inside = lax.rem(place, 16) < ZL
-    target = jnp.where(inside, (place // 16) * ZL + lax.rem(place, 16), -2).astype(F32)
-    onehot = jnp.where(target == cell_row, 1.0, 0.0).astype(BF16)
+    place = iota((192, slots), 0)
+    slot = iota((192, slots), 1) // CAP
+    group = jnp.where(slot >= LEFT, 2, jnp.where(slot >= RIGHT, 1, 0))
+    inside = (lax.rem(place, 16) < ZL) & (place // 64 == group)
+    target = jnp.where(inside, lax.rem(place, 64) // 16 * ZL + lax.rem(place, 16), -2)
+    onehot = jnp.where(target.astype(F32) == cell_row, 1.0, 0.0).astype(BF16)
     r_hi, r_lo = split(wrecv[:, 0:CAP, :].reshape(slots, 128))
-    wall = dot(onehot, r_hi) + dot(onehot, r_lo)
-    xsend[...] = wall.reshape(XL, 16, 128)
+    wall = (dot(onehot, r_hi) + dot(onehot, r_lo)).reshape(3, XL, 16, 128)
+    dsend[...] = wall[1:3, :, 0:ZL, :]
+    sums = [
+        remote(dsend.at[0], drecv.at[0], d_send.at[0], d_recv.at[0], gx, at(4, y)),
+        remote(dsend.at[1], drecv.at[1], d_send.at[1], d_recv.at[1], gx, at(-4, y)),
+    ]
+    for c in sums:
+        c.start()
+    pl.semaphore_wait(known, 2)
+    fields_at(NEAR + 1, 8, range(XL))
+    for x in range(XL):
+        send_field(8, x)
+    loads[4].wait()
+    m_hi, m_lo = split(m_f32[...])
+    mh[...] = m_hi
+    ml[...] = m_lo
+
+    for c in sums:
+        c.wait_recv()
+    xsend[...] = wall[0, :, 0:ZL, :] + drecv[0] + drecv[1]
     for k in range(1, GY):
         other = lax.rem(y + k, GY)
         remote(
@@ -187,7 +252,8 @@
     xrecv[y] = xsend[y]
     for k in range(1, GY):
         pltpu.make_async_copy(xsend.at[0], xrecv.at[0], x_recv.at[k - 1]).wait()
-    wall_t = jnp.transpose(xrecv[...].reshape(64, 128))
+    given = jnp.concatenate([xrecv[...], jnp.zeros((GY, 16 - ZL, 128), F32)], axis=1)
+    wall_t = jnp.transpose(given.reshape(64, 128))
     p = iota((64, 192), 0)
     col = iota((64, 192), 1)
     forcing = jnp.zeros((KW, 192), F32)
@@ -234,7 +300,9 @@
 
     for h in halos:
         h.wait_send()
-    pltpu.make_async_copy(wsend.at[others], wrecv.at[others], w_send).wait()
+    pltpu.make_async_copy(wsend.at[got_wall], wrecv.at[got_wall], w_send).wait()
+    for c in sums:
+        c.wait_send()
     pltpu.make_async_copy(fsend.at[others], frecv.at[others], f_send).wait()
     pltpu.make_async_copy(bsend.at[others], brecv.at[others], b_send).wait()
     for k in range(1, GY):
@@ -242,7 +310,7 @@
 
 
 def on_device(adjoint, velocity, shear, matrix, rows, cells, counts):
-    anywhere = pl.BlockSpec(memory_space=pl.ANY)
+    anywhere = pl.BlockSpec(memory_space=pltpu.HBM)
     smem = pl.BlockSpec(memory_space=pltpu.SMEM)
     vmem = pltpu.VMEM
     dma = pltpu.SemaphoreType.DMA
@@ -258,20 +326,23 @@
             vmem((NY, NY), F32),
             vmem((NY, NY), BF16),
             vmem((NY, NY), BF16),
-            vmem((NGZ, CAP), jnp.int32),
+            vmem((CAP, NGZ), jnp.int32),
             vmem((1, NGZ), jnp.int32),
             vmem((NGZ, CAP + 1, 128), F32),
             vmem((NGZ, CAP + 1, 128), F32),
             message, message, message, message,
-            vmem((GY, 16, 128), F32),
-            vmem((GY, 16, 128), F32),
-            dma((5,)), dma((2,)), dma((2,)), dma, dma, dma, dma, dma, dma, dma((3,)), dma((3,)),
+            vmem((GY, ZL, 128), F32),
+            vmem((GY, ZL, 128), F32),
+            vmem((2, XL, ZL, 128), F32),
+            vmem((2, XL, ZL, 128), F32),
+            dma((5,)), dma((2,)), dma((2,)), dma, dma, dma, dma, dma, dma, dma((3,)), dma((3,)), dma((2,)), dma((2,)),
+            pltpu.SemaphoreType.REGULAR,
         ],
         compiler_params=pltpu.CompilerParams(
-            collective_id=0, has_side_effects=True, vmem_limit_bytes=48 * 1024 * 1024
+            collective_id=0, has_side_effects=True, vmem_limit_bytes=64 * 1024 * 1024
         ),
         cost_estimate=pl.CostEstimate(flops=310_000_000, bytes_accessed=3_000_000, transcendentals=0),
-    )(adjoint, velocity, shear, matrix, rows, cells, counts)
+    )(adjoint, velocity, shear, matrix, rows, jnp.swapaxes(cells, 2, 3), counts)
 
 
 def solution(mesh):

time: 77.6 us -> 67.5 us (0.87); the launches traced: 77.3 us -> 66.3 us
  Pallas kernels: 72.5 us -> 64.6 us
  local copies, waits for them, and re-layouts: 4.73 us -> 1.77 us
    pallas_call x1, Pallas kernels: 72.5 us -> 64.6 us  [on_device(): pl.pallas_call(kernel, out_shape=jax.ShapeDtypeStruct((F, XL, LEV, NZ), F...]
    unnamed x14 -> x1, local copies, waits for them, and re-layouts: 4.73 us -> 1.77 us
where the time goes in v1:
time: 67.5 us; the launch traced here: 66.3 us
  Pallas kernels  64.6 us (96%)
  local copies, waits for them, and re-layouts  1.77 us (3%)
    pallas_call x1, Pallas kernels, on_device(): pl.pallas_call(kernel, out_shape=jax.ShapeDtypeStruct((F, XL, LEV, NZ), F...  64.6 us
    unnamed x1, local copies, waits for them, and re-layouts  1.77 us

profile of v1, /device:TPU:6, one launch (start us, length us, event | category | flops | bytes accessed | tf_op | source)
XLA Modules:
  0.0 66.3 jit_solution(13911144925150947185)
XLA Ops:
  0.0 64.6 %shard_map.73 = f32[4,4,8,768]{3,2,1,0:T(8,128)} custom-call(f32[4,4,8,768]{3,2,1,0:T(8,128)} %adj_hbm.1, f32[8]{0:T(128)} %vel_ref.1, f32[8]{0:T(128)} %shear_ref.1, f32[512,512]{1,0:T(8,128)} %m_hbm.1, f32[1,1,64,8,128]{4,3,2,1,0:T(8,128)} %rows_hbm.1, s32[1,1,8,64]{3,2,1,0:T(8,128)} %bitcast.1, s32[1,1,64]{2,1,0:T(1,128)} %counts_hbm.1), custom_call_target="tpu_custom_call" | custom-call | flops 310000000 | bytes 3000000 | tf_op jit(solution)/shard_map/pallas_call | solution.py:318
  64.6 1.8 %copy.9 = f32[4,4,8,768]{3,2,1,0:T(8,128)} copy(f32[4,4,8,768]{3,2,1,0:T(8,128)} %shard_map.73) | data formatting | bytes 786432

commit v2 on v1

--- a/solution.py
+++ b/solution.py
@@ -48,8 +48,8 @@
 def kernel(
     adj_hbm, vel_ref, shear_ref, m_hbm, rows_hbm, cells_hbm, counts_hbm,
     out_ref,
-    adj, halo, m_f32, mh, ml, cells, counts, wsend, wrecv, fsend, frecv, bsend, brecv, xsend, xrecv, dsend, drecv,
-    local_sem, halo_send, halo_recv, w_send, w_recv, f_send, f_recv, b_send, b_recv, x_send, x_recv, d_send, d_recv, known,
+    adj, halo, m_f32, mh, ml, cells, counts, wsend, wrecv, fsend, frecv, bsend, brecv, fsend2, frecv2, bsend2, brecv2, xsend, xrecv, dsend, drecv,
+    local_sem, halo_send, halo_recv, w_send, w_recv, f_send, f_recv, b_send, b_recv, f_send2, f_recv2, b_send2, b_recv2, x_send, x_recv, d_send, d_recv, known,
 ):
     gx = lax.axis_index("gx")
     me = lax.axis_index("gz")
@@ -122,8 +122,8 @@
             rows.append(e)
         for w in range(GZ):
             first, second = pack(rows, w)
-            fsend[w * GY + x, 0:8, :] = first
-            fsend[w * GY + x, 8:12, :] = second
+            fsend[w * GY + x] = first
+            fsend2[w * GY + x] = second
 
     loads[0].wait()
     step_and_pack(1)
@@ -144,9 +144,13 @@
         owner, dest = at(owner_dz, iy), at(dz, iy)
         remote(wsend.at[owner], wrecv.at[slot], w_send, w_recv, gx, dest).start()
 
-    def send_field(dz, x):
+    def send_first(dz, x):
         dest = at(dz, x)
         remote(fsend.at[dest], frecv.at[me], f_send, f_recv, gx, dest).start()
+
+    def send_second(dz, x):
+        dest = at(dz, x)
+        remote(fsend2.at[dest], frecv2.at[me], f_send2, f_recv2, gx, dest).start()
 
     def wall_here(k, c):
         iy = lax.rem(y + k, GY)
@@ -182,31 +186,32 @@
 
     lax.fori_loop(0, GY, wall_8, 0)
 
-    def fields_at(first, last, xs):
+    def fields_at(send, first, last, xs):
         def body(level, c):
             for x in xs:
-                send_field(level, x)
-                send_field(-level, x)
+                send(level, x)
+                send(-level, x)
             return c
 
         lax.fori_loop(first, last, body, 0)
 
-    def fields_here(xs):
+    def fields_here(send, xs):
         for x in xs:
 
             @pl.when(x != y)
             def _():
-                send_field(0, x)
-
-    fields_at(1, NEAR + 1, (1, 2))
-    fields_here((1, 2))
+                send(0, x)
+
+    fields_at(send_first, 1, NEAR + 1, (1, 2))
+    fields_here(send_first, (1, 2))
     for h in halos:
         h.wait_recv()
     step_and_pack(0)
     step_and_pack(3)
-    fields_at(1, NEAR + 1, (0, 3))
-    fields_here((0, 3))
+    fields_at(send_first, 1, NEAR + 1, (0, 3))
+    fields_here(send_first, (0, 3))
     frecv[me] = fsend[me]
+    frecv2[me] = fsend2[me]
 
     others = pl.ds(0, NGZ - 1)
     got_wall = pl.ds(0, NGZ - 3)
@@ -233,9 +238,20 @@
     for c in sums:
         c.start()
     pl.semaphore_wait(known, 2)
-    fields_at(NEAR + 1, 8, range(XL))
+    fields_at(send_first, NEAR + 1, 8, range(XL))
     for x in range(XL):
-        send_field(8, x)
+        send_first(8, x)
+    for x in range(XL):
+        send_second(8, x)
+
+    def second_at(k, c):
+        for x in range(XL):
+            send_second(8 - k, x)
+            send_second(k - 8, x)
+        return c
+
+    lax.fori_loop(1, 8, second_at, 0)
+    fields_here(send_second, range(XL))
     loads[4].wait()
     m_hi, m_lo = split(m_f32[...])
     mh[...] = m_hi
@@ -263,40 +279,58 @@
         v_hi, v_lo = split(wall_t[KW * f : KW * (f + 1)])
         forcing = forcing + dot(v_hi, there) + dot(v_lo, there)
 
+    def product(columns, part):
+        top = columns[0:KW] + forcing[:, part]
+        c_hi, c_lo = split(jnp.concatenate([top, columns[KW:]], axis=0))
+        return dot(mh[...], c_hi) + dot(mh[...], c_lo) + dot(ml[...], c_hi)
+
+    def send_back(src, dst, ss, rs):
+        def back(dest):
+            remote(src.at[dest], dst.at[me], ss, rs, gx, dest).start()
+
+        for iy in range(GY):
+            back(at(8, iy))
+
+        def body(k, c):
+            for iy in range(GY):
+                back(at(8 - k, iy))
+                back(at(k - 8, iy))
+            return c
+
+        lax.fori_loop(1, 8, body, 0)
+        for k in range(1, GY):
+            back(at(0, lax.rem(y + k, GY)))
+        dst[me] = src[me]
+
     pltpu.make_async_copy(fsend.at[others], frecv.at[others], f_recv).wait()
-    left = frecv[:, 0:8, :].reshape(NY, 128)
-    tail = frecv[:, 8:12, :]
-    right = jnp.concatenate([tail[:, :, 0:64], tail[:, :, 64:128]], axis=1).reshape(NY, 64)
-    columns = jnp.concatenate([left, right], axis=1)
-    columns = jnp.concatenate([columns[0:KW] + forcing, columns[KW:]], axis=0)
-    c_hi, c_lo = split(columns)
-    solved = dot(mh[...], c_hi) + dot(mh[...], c_lo) + dot(ml[...], c_hi)
-    bsend[:, 0:8, :] = solved[:, 0:128].reshape(NGZ, LEV, 128)
-    back = solved[:, 128:192].reshape(NGZ, LEV, 64)
-    bsend[:, 8:12, :] = jnp.concatenate([back[:, 0:4, :], back[:, 4:8, :]], axis=2)
-
-    def send_back(i, c):
-        d = lax.rem(me + i, NGZ)
-        remote(bsend.at[d], brecv.at[me], b_send, b_recv, gx, d).start()
-        return c
-
-    lax.fori_loop(1, NGZ, send_back, 0)
-    brecv[me] = bsend[me]
+    left = product(frecv[...].reshape(NY, 128), slice(0, 128))
+    bsend[...] = left.reshape(NGZ, LEV, 128)
+    send_back(bsend, brecv, b_send, b_recv)
+
+    pltpu.make_async_copy(fsend2.at[others], frecv2.at[others], f_recv2).wait()
+    tail = frecv2[...]
+    tail = jnp.concatenate([tail[:, :, 0:64], tail[:, :, 64:128]], axis=1)
+    right = product(tail.reshape(NY, 64), slice(128, 192)).reshape(NGZ, LEV, 64)
+    bsend2[...] = jnp.concatenate([right[:, 0:4, :], right[:, 4:8, :]], axis=2)
+    send_back(bsend2, brecv2, b_send2, b_recv2)
+
     pltpu.make_async_copy(bsend.at[others], brecv.at[others], b_recv).wait()
-
     for x in range(XL):
-        pieces = [[] for _ in range(F)]
+        for f in range(2):
+            out_ref[f, x] = jnp.concatenate(
+                [brecv[w * GY + x, :, WIN * f : WIN * (f + 1)] for w in range(GZ)], axis=1
+            )
+    pltpu.make_async_copy(bsend2.at[others], brecv2.at[others], b_recv2).wait()
+    for x in range(XL):
+        pieces = [[], []]
         for w in range(GZ):
-            b0 = brecv[w * GY + x, 0:8, :]
-            b1 = brecv[w * GY + x, 8:12, :]
+            b0 = brecv[w * GY + x]
+            b1 = brecv2[w * GY + x]
             b1 = jnp.concatenate([b1[:, 0:64], b1[:, 64:128]], axis=0)
-            pieces[0].append(b0[:, 0:48])
-            pieces[1].append(b0[:, 48:96])
-            pieces[2].append(b0[:, 96:128])
-            pieces[2].append(b1[:, 0:16])
-            pieces[3].append(b1[:, 16:64])
-        for f in range(F):
-            out_ref[f, x] = jnp.concatenate(pieces[f], axis=1)
+            pieces[0] += [b0[:, 96:128], b1[:, 0:16]]
+            pieces[1].append(b1[:, 16:64])
+        out_ref[2, x] = jnp.concatenate(pieces[0], axis=1)
+        out_ref[3, x] = jnp.concatenate(pieces[1], axis=1)
 
     for h in halos:
         h.wait_send()
@@ -305,6 +339,8 @@
         c.wait_send()
     pltpu.make_async_copy(fsend.at[others], frecv.at[others], f_send).wait()
     pltpu.make_async_copy(bsend.at[others], brecv.at[others], b_send).wait()
+    pltpu.make_async_copy(fsend2.at[others], frecv2.at[others], f_send2).wait()
+    pltpu.make_async_copy(bsend2.at[others], brecv2.at[others], b_send2).wait()
     for k in range(1, GY):
         pltpu.make_async_copy(xsend.at[0], xrecv.at[0], x_send.at[k - 1]).wait()
 
@@ -314,7 +350,7 @@
     smem = pl.BlockSpec(memory_space=pltpu.SMEM)
     vmem = pltpu.VMEM
     dma = pltpu.SemaphoreType.DMA
-    message = vmem((NGZ, ROWS, 128), F32)
+    first, second = vmem((NGZ, 8, 128), F32), vmem((NGZ, 4, 128), F32)
     return pl.pallas_call(
         kernel,
         out_shape=jax.ShapeDtypeStruct((F, XL, LEV, NZ), F32),
@@ -330,12 +366,12 @@
             vmem((1, NGZ), jnp.int32),
             vmem((NGZ, CAP + 1, 128), F32),
             vmem((NGZ, CAP + 1, 128), F32),
-            message, message, message, message,
+            first, first, first, first, second, second, second, second,
             vmem((GY, ZL, 128), F32),
             vmem((GY, ZL, 128), F32),
             vmem((2, XL, ZL, 128), F32),
             vmem((2, XL, ZL, 128), F32),
-            dma((5,)), dma((2,)), dma((2,)), dma, dma, dma, dma, dma, dma, dma((3,)), dma((3,)), dma((2,)), dma((2,)),
+            dma((5,)), dma((2,)), dma((2,)), *[dma] * 10, dma((3,)), dma((3,)), dma((2,)), dma((2,)),
             pltpu.SemaphoreType.REGULAR,
         ],
         compiler_params=pltpu.CompilerParams(

time: 67.5 us -> 64.6 us (0.957)
  Pallas kernels: 64.6 us -> 61.9 us
    pallas_call x1, Pallas kernels: 64.6 us -> 61.9 us  [on_device(): pl.pallas_call(kernel, out_shape=jax.ShapeDtypeStruct((F, XL, LEV, NZ), F...]
where the time goes in v2:
time: 64.6 us; the launch traced here: 63.7 us
  Pallas kernels  61.9 us (96%)
  local copies, waits for them, and re-layouts  1.77 us (3%)
    pallas_call x1, Pallas kernels, on_device(): pl.pallas_call(kernel, out_shape=jax.ShapeDtypeStruct((F, XL, LEV, NZ), F...  61.9 us
    unnamed x1, local copies, waits for them, and re-layouts  1.77 us

profile of v2, /device:TPU:6, one launch (start us, length us, event | category | flops | bytes accessed | tf_op | source)
XLA Modules:
  0.0 63.7 jit_solution(12065857898071593907)
XLA Ops:
  0.0 61.9 %shard_map.73 = f32[4,4,8,768]{3,2,1,0:T(8,128)} custom-call(f32[4,4,8,768]{3,2,1,0:T(8,128)} %adj_hbm.1, f32[8]{0:T(128)} %vel_ref.1, f32[8]{0:T(128)} %shear_ref.1, f32[512,512]{1,0:T(8,128)} %m_hbm.1, f32[1,1,64,8,128]{4,3,2,1,0:T(8,128)} %rows_hbm.1, s32[1,1,8,64]{3,2,1,0:T(8,128)} %bitcast.1, s32[1,1,64]{2,1,0:T(1,128)} %counts_hbm.1), custom_call_target="tpu_custom_call" | custom-call | flops 310000000 | bytes 3000000 | tf_op jit(solution)/shard_map/pallas_call | solution.py:354
  61.9 1.8 %copy.9 = f32[4,4,8,768]{3,2,1,0:T(8,128)} copy(f32[4,4,8,768]{3,2,1,0:T(8,128)} %shard_map.73) | data formatting | bytes 786432

commit v3 on v2

--- a/solution.py
+++ b/solution.py
@@ -20,7 +20,6 @@
 KW = 32
 NEAR = 4
 DIRECT, RIGHT, LEFT = 0, 28, 46
-ROWS = 12
 
 
 def iota(shape, dim):
@@ -47,9 +46,9 @@
 
 def kernel(
     adj_hbm, vel_ref, shear_ref, m_hbm, rows_hbm, cells_hbm, counts_hbm,
-    out_ref,
-    adj, halo, m_f32, mh, ml, cells, counts, wsend, wrecv, fsend, frecv, bsend, brecv, fsend2, frecv2, bsend2, brecv2, xsend, xrecv, dsend, drecv,
-    local_sem, halo_send, halo_recv, w_send, w_recv, f_send, f_recv, b_send, b_recv, f_send2, f_recv2, b_send2, b_recv2, x_send, x_recv, d_send, d_recv, known,
+    brecv, brecv2,
+    adj, halo, m_f32, mh, ml, cells, counts, wsend, wrecv, fsend, frecv, bsend, fsend2, frecv2, bsend2, xsend, xrecv,
+    local_sem, halo_send, halo_recv, w_send, w_recv, f_send, f_recv, b_send, b_recv, f_send2, f_recv2, b_send2, b_recv2, x_send, x_recv, known,
 ):
     gx = lax.axis_index("gx")
     me = lax.axis_index("gz")
@@ -133,10 +132,12 @@
     signal(known, gx, at(NEAR, y))
     signal(known, gx, at(-NEAR, y))
 
-    halos = [
-        remote(adj.at[:, XL - 1], halo.at[0], halo_send.at[0], halo_recv.at[0], after, me),
-        remote(adj.at[:, 0], halo.at[1], halo_send.at[1], halo_recv.at[1], before, me),
-    ]
+    halos = []
+    for f in range(F):
+        halos += [
+            remote(adj.at[f, XL - 1], halo.at[0, f], halo_send.at[0], halo_recv.at[0], after, me),
+            remote(adj.at[f, 0], halo.at[1, f], halo_send.at[1], halo_recv.at[1], before, me),
+        ]
     for h in halos:
         h.start()
 
@@ -204,8 +205,8 @@
 
     fields_at(send_first, 1, NEAR + 1, (1, 2))
     fields_here(send_first, (1, 2))
-    for h in halos:
-        h.wait_recv()
+    for k in range(2):
+        pltpu.make_async_copy(halo.at[k], halo.at[k], halo_recv.at[k]).wait()
     step_and_pack(0)
     step_and_pack(3)
     fields_at(send_first, 1, NEAR + 1, (0, 3))
@@ -213,6 +214,10 @@
     frecv[me] = fsend[me]
     frecv2[me] = fsend2[me]
 
+    pl.semaphore_wait(known, 2)
+    fields_at(send_first, NEAR + 1, 8, range(XL))
+    for x in range(XL):
+        send_first(8, x)
     others = pl.ds(0, NGZ - 1)
     got_wall = pl.ds(0, NGZ - 3)
     pltpu.make_async_copy(wsend.at[got_wall], wrecv.at[got_wall], w_recv).wait()
@@ -229,18 +234,23 @@
     target = jnp.where(inside, lax.rem(place, 64) // 16 * ZL + lax.rem(place, 16), -2)
     onehot = jnp.where(target.astype(F32) == cell_row, 1.0, 0.0).astype(BF16)
     r_hi, r_lo = split(wrecv[:, 0:CAP, :].reshape(slots, 128))
-    wall = (dot(onehot, r_hi) + dot(onehot, r_lo)).reshape(3, XL, 16, 128)
-    dsend[...] = wall[1:3, :, 0:ZL, :]
-    sums = [
-        remote(dsend.at[0], drecv.at[0], d_send.at[0], d_recv.at[0], gx, at(4, y)),
-        remote(dsend.at[1], drecv.at[1], d_send.at[1], d_recv.at[1], gx, at(-4, y)),
-    ]
-    for c in sums:
-        c.start()
-    pl.semaphore_wait(known, 2)
-    fields_at(send_first, NEAR + 1, 8, range(XL))
-    for x in range(XL):
-        send_first(8, x)
+    wall = (dot(onehot, r_hi) + dot(onehot, r_lo)).reshape(3 * XL, 16, 128)
+    xsend[...] = wall[:, 0:ZL]
+
+    def send_sums(xc, c):
+        there = gx, at(4, xc)
+        remote(xsend.at[4 + xc], xrecv.at[4 + y], x_send, x_recv, *there).start()
+        there = gx, at(-4, xc)
+        remote(xsend.at[8 + xc], xrecv.at[8 + y], x_send, x_recv, *there).start()
+
+        @pl.when(xc != y)
+        def _():
+            remote(xsend.at[xc], xrecv.at[y], x_send, x_recv, gx, at(0, xc)).start()
+
+        return c
+
+    lax.fori_loop(0, XL, send_sums, 0)
+    xrecv[y] = xsend[y]
     for x in range(XL):
         send_second(8, x)
 
@@ -257,18 +267,10 @@
     mh[...] = m_hi
     ml[...] = m_lo
 
-    for c in sums:
-        c.wait_recv()
-    xsend[...] = wall[0, :, 0:ZL, :] + drecv[0] + drecv[1]
-    for k in range(1, GY):
-        other = lax.rem(y + k, GY)
-        remote(
-            xsend.at[other], xrecv.at[y], x_send.at[k - 1], x_recv.at[k - 1], gx, z * GY + other
-        ).start()
-    xrecv[y] = xsend[y]
-    for k in range(1, GY):
-        pltpu.make_async_copy(xsend.at[0], xrecv.at[0], x_recv.at[k - 1]).wait()
-    given = jnp.concatenate([xrecv[...], jnp.zeros((GY, 16 - ZL, 128), F32)], axis=1)
+    eleven = pl.ds(0, 3 * XL - 1)
+    pltpu.make_async_copy(xsend.at[eleven], xrecv.at[eleven], x_recv).wait()
+    sums = xrecv[0:GY] + xrecv[GY : 2 * GY] + xrecv[2 * GY :]
+    given = jnp.concatenate([sums, jnp.zeros((GY, 16 - ZL, 128), F32)], axis=1)
     wall_t = jnp.transpose(given.reshape(64, 128))
     p = iota((64, 192), 0)
     col = iota((64, 192), 1)
@@ -279,6 +281,10 @@
         v_hi, v_lo = split(wall_t[KW * f : KW * (f + 1)])
         forcing = forcing + dot(v_hi, there) + dot(v_lo, there)
 
+    own = [
+        pltpu.make_async_copy(bsend.at[me], brecv.at[me], local_sem.at[0]),
+        pltpu.make_async_copy(bsend2.at[me], brecv2.at[me], local_sem.at[1]),
+    ]
     def product(columns, part):
         top = columns[0:KW] + forcing[:, part]
         c_hi, c_lo = split(jnp.concatenate([top, columns[KW:]], axis=0))
@@ -300,12 +306,12 @@
         lax.fori_loop(1, 8, body, 0)
         for k in range(1, GY):
             back(at(0, lax.rem(y + k, GY)))
-        dst[me] = src[me]
 
     pltpu.make_async_copy(fsend.at[others], frecv.at[others], f_recv).wait()
     left = product(frecv[...].reshape(NY, 128), slice(0, 128))
     bsend[...] = left.reshape(NGZ, LEV, 128)
     send_back(bsend, brecv, b_send, b_recv)
+    own[0].start()
 
     pltpu.make_async_copy(fsend2.at[others], frecv2.at[others], f_recv2).wait()
     tail = frecv2[...]
@@ -313,36 +319,51 @@
     right = product(tail.reshape(NY, 64), slice(128, 192)).reshape(NGZ, LEV, 64)
     bsend2[...] = jnp.concatenate([right[:, 0:4, :], right[:, 4:8, :]], axis=2)
     send_back(bsend2, brecv2, b_send2, b_recv2)
+    own[1].start()
 
     pltpu.make_async_copy(bsend.at[others], brecv.at[others], b_recv).wait()
-    for x in range(XL):
-        for f in range(2):
-            out_ref[f, x] = jnp.concatenate(
-                [brecv[w * GY + x, :, WIN * f : WIN * (f + 1)] for w in range(GZ)], axis=1
-            )
     pltpu.make_async_copy(bsend2.at[others], brecv2.at[others], b_recv2).wait()
-    for x in range(XL):
-        pieces = [[], []]
-        for w in range(GZ):
-            b0 = brecv[w * GY + x]
-            b1 = brecv2[w * GY + x]
-            b1 = jnp.concatenate([b1[:, 0:64], b1[:, 64:128]], axis=0)
-            pieces[0] += [b0[:, 96:128], b1[:, 0:16]]
-            pieces[1].append(b1[:, 16:64])
-        out_ref[2, x] = jnp.concatenate(pieces[0], axis=1)
-        out_ref[3, x] = jnp.concatenate(pieces[1], axis=1)
-
-    for h in halos:
-        h.wait_send()
+    for c in own:
+        c.wait()
+    for k in range(2):
+        pltpu.make_async_copy(halo.at[k], halo.at[k], halo_send.at[k]).wait()
     pltpu.make_async_copy(wsend.at[got_wall], wrecv.at[got_wall], w_send).wait()
-    for c in sums:
-        c.wait_send()
+    pltpu.make_async_copy(xsend.at[eleven], xrecv.at[eleven], x_send).wait()
     pltpu.make_async_copy(fsend.at[others], frecv.at[others], f_send).wait()
     pltpu.make_async_copy(bsend.at[others], brecv.at[others], b_send).wait()
     pltpu.make_async_copy(fsend2.at[others], frecv2.at[others], f_send2).wait()
     pltpu.make_async_copy(bsend2.at[others], brecv2.at[others], b_send2).wait()
-    for k in range(1, GY):
-        pltpu.make_async_copy(xsend.at[0], xrecv.at[0], x_send.at[k - 1]).wait()
+
+
+def unpack(first, second, out, got, got2, done, in_sem, out_sem):
+    loads = []
+    for x in range(XL):
+        loads.append(
+            (
+                pltpu.make_async_copy(first.at[:, x], got.at[x], in_sem.at[0, x]),
+                pltpu.make_async_copy(second.at[:, x], got2.at[x], in_sem.at[1, x]),
+            )
+        )
+        for load in loads[x]:
+            load.start()
+    stores = [pltpu.make_async_copy(done.at[:, x], out.at[:, x], out_sem.at[x]) for x in range(XL)]
+    for x in range(XL):
+        for load in loads[x]:
+            load.wait()
+        pieces = [[] for _ in range(F)]
+        for w in range(GZ):
+            b0 = got[x, w]
+            b1 = got2[x, w]
+            b1 = jnp.concatenate([b1[:, 0:64], b1[:, 64:128]], axis=0)
+            pieces[0].append(b0[:, 0:48])
+            pieces[1].append(b0[:, 48:96])
+            pieces[2] += [b0[:, 96:128], b1[:, 0:16]]
+            pieces[3].append(b1[:, 16:64])
+        for f in range(F):
+            done[f, x] = jnp.concatenate(pieces[f], axis=1)
+        stores[x].start()
+    for store in stores:
+        store.wait()
 
 
 def on_device(adjoint, velocity, shear, matrix, rows, cells, counts):
@@ -351,11 +372,11 @@
     vmem = pltpu.VMEM
     dma = pltpu.SemaphoreType.DMA
     first, second = vmem((NGZ, 8, 128), F32), vmem((NGZ, 4, 128), F32)
-    return pl.pallas_call(
+    back = pl.pallas_call(
         kernel,
-        out_shape=jax.ShapeDtypeStruct((F, XL, LEV, NZ), F32),
+        out_shape=[jax.ShapeDtypeStruct((NGZ, r, 128), F32) for r in (8, 4)],
         in_specs=[anywhere, smem, smem, anywhere, anywhere, anywhere, anywhere],
-        out_specs=pl.BlockSpec(memory_space=pltpu.VMEM),
+        out_specs=[anywhere, anywhere],
         scratch_shapes=[
             vmem((F, XL, LEV, NZ), F32),
             vmem((2, F, LEV, NZ), F32),
@@ -366,12 +387,10 @@
             vmem((1, NGZ), jnp.int32),
             vmem((NGZ, CAP + 1, 128), F32),
             vmem((NGZ, CAP + 1, 128), F32),
-            first, first, first, first, second, second, second, second,
-            vmem((GY, ZL, 128), F32),
-            vmem((GY, ZL, 128), F32),
-            vmem((2, XL, ZL, 128), F32),
-            vmem((2, XL, ZL, 128), F32),
-            dma((5,)), dma((2,)), dma((2,)), *[dma] * 10, dma((3,)), dma((3,)), dma((2,)), dma((2,)),
+            first, first, first, second, second, second,
+            vmem((3 * XL, ZL, 128), F32),
+            vmem((3 * GY, ZL, 128), F32),
+            dma((5,)), dma((2,)), dma((2,)), *[dma] * 12,
             pltpu.SemaphoreType.REGULAR,
         ],
         compiler_params=pltpu.CompilerParams(
@@ -379,6 +398,21 @@
         ),
         cost_estimate=pl.CostEstimate(flops=310_000_000, bytes_accessed=3_000_000, transcendentals=0),
     )(adjoint, velocity, shear, matrix, rows, jnp.swapaxes(cells, 2, 3), counts)
+
+    return pl.pallas_call(
+        unpack,
+        out_shape=jax.ShapeDtypeStruct((F, XL, LEV, NZ), F32),
+        in_specs=[anywhere, anywhere],
+        out_specs=anywhere,
+        scratch_shapes=[
+            vmem((XL, GZ, 8, 128), F32),
+            vmem((XL, GZ, 4, 128), F32),
+            vmem((F, XL, LEV, NZ), F32),
+            dma((2, XL)),
+            dma((XL,)),
+        ],
+        compiler_params=pltpu.CompilerParams(vmem_limit_bytes=64 * 1024 * 1024),
+    )(*(b.reshape(GZ, GY, b.shape[1], 128) for b in back))
 
 
 def solution(mesh):

time: 64.6 us -> 63.5 us (0.983)
  local copies, waits for them, and re-layouts: 1.77 us -> 0 us
  Pallas kernels: 61.9 us -> 63.2 us
    unnamed x1 -> x0, local copies, waits for them, and re-layouts: 1.77 us -> none
    pallas_call x1 -> x2, Pallas kernels: 61.9 us -> 63.2 us  [the longest x1 60.9 us: on_device(): pl.pallas_call(kernel, out_shape=[jax.ShapeDtypeStruct((NGZ, r, 128), F32...]
where the time goes in v3:
time: 63.5 us; the launch traced here: 63.2 us
  Pallas kernels  63.2 us (100%)
    pallas_call x1, Pallas kernels, on_device(): pl.pallas_call(kernel, out_shape=[jax.ShapeDtypeStruct((NGZ, r, 128), F32...  60.9 us
    pallas_call x1, Pallas kernels, on_device(): pl.pallas_call(unpack, out_shape=jax.ShapeDtypeStruct((F, XL, LEV, NZ), F...  2.31 us

profile of v3, /device:TPU:6, one launch (start us, length us, event | category | flops | bytes accessed | tf_op | source)
XLA Modules:
  0.0 63.2 jit_solution(11226022029425076985)
XLA Ops:
  0.0 60.9 %shard_map.73 = (f32[64,8,128]{2,1,0:T(8,128)}, f32[64,4,128]{2,1,0:T(4,128)}) custom-call(f32[4,4,8,768]{3,2,1,0:T(8,128)} %adj_hbm.1, f32[8]{0:T(128)} %vel_ref.1, f32[8]{0:T(128)} %shear_ref.1, f32[512,512]{1,0:T(8,128)} %m_hbm.1, f32[1,1,64,8,128]{4,3,2,1,0:T(8,128)} %rows_hbm.1, s32[1,1,8,64]{3,2,1,0:T(8,128)} %bitcast.5, s32[1,1,64]{2,1,0:T(1,128)} %counts_hbm.1), custom_call_target="tpu_custom_call" | custom-call | flops 310000000 | bytes 3000000 | tf_op jit(solution)/shard_map/pallas_call | solution.py:375
  60.9 2.3 %shard_map.74 = f32[4,4,8,768]{3,2,1,0:T(8,128)} custom-call(f32[16,4,8,128]{3,2,1,0:T(8,128)} %bitcast.3, f32[16,4,4,128]{3,2,1,0:T(4,128)} %bitcast.4), custom_call_target="tpu_custom_call" | custom-call | tf_op jit(solution)/shard_map/pallas_call | solution.py:402

commit v4 on v3

--- a/solution.py
+++ b/solution.py
@@ -48,7 +48,7 @@
     adj_hbm, vel_ref, shear_ref, m_hbm, rows_hbm, cells_hbm, counts_hbm,
     brecv, brecv2,
     adj, halo, m_f32, mh, ml, cells, counts, wsend, wrecv, fsend, frecv, bsend, fsend2, frecv2, bsend2, xsend, xrecv,
-    local_sem, halo_send, halo_recv, w_send, w_recv, f_send, f_recv, b_send, b_recv, f_send2, f_recv2, b_send2, b_recv2, x_send, x_recv, known,
+    local_sem, halo_send, halo_recv, w_send, w_recv, s_recv, f_send, f_recv, b_send, b_recv, f_send2, f_recv2, b_send2, b_recv2, x_send, x_recv, known,
 ):
     gx = lax.axis_index("gx")
     me = lax.axis_index("gz")
@@ -65,23 +65,6 @@
 
     def signal(sem, ix, iz):
         pl.semaphore_signal(sem, inc=1, device_id=(ix, iz), device_id_type=MESH)
-
-    barrier = pltpu.get_barrier_semaphore()
-    after, before = lax.rem(gx + 1, NGX), lax.rem(gx + NGX - 1, NGX)
-    signal(barrier, after, me)
-    signal(barrier, before, me)
-
-    def greet_here(k, c):
-        signal(barrier, gx, at(0, lax.rem(y + k, GY)))
-        return c
-
-    def greet_near(k, c):
-        signal(barrier, gx, at(NEAR - k // GY, lax.rem(k, GY)))
-        signal(barrier, gx, at(k // GY - NEAR, lax.rem(k, GY)))
-        return c
-
-    lax.fori_loop(1, GY, greet_here, 0)
-    lax.fori_loop(0, NEAR * GY, greet_near, 0)
 
     loads = [
         pltpu.make_async_copy(adj_hbm, adj, local_sem.at[0]),
@@ -92,6 +75,24 @@
     ]
     for load in loads:
         load.start()
+
+    barrier = pltpu.get_barrier_semaphore()
+    after, before = lax.rem(gx + 1, NGX), lax.rem(gx + NGX - 1, NGX)
+    signal(barrier, after, me)
+    signal(barrier, before, me)
+
+    def greet_here(k, c):
+        signal(barrier, gx, at(0, lax.rem(y + k, GY)))
+        return c
+
+    def greet_near(k, c):
+        signal(barrier, gx, at(NEAR - k // GY, lax.rem(k, GY)))
+        signal(barrier, gx, at(k // GY - NEAR, lax.rem(k, GY)))
+        return c
+
+    lax.fori_loop(1, GY, greet_here, 0)
+    lax.fori_loop(0, NEAR * GY, greet_near, 0)
+
 
     loads[1].wait()
     loads[2].wait()
@@ -141,9 +142,9 @@
     for h in halos:
         h.start()
 
-    def send_wall(owner_dz, dz, iy, slot):
+    def send_wall(owner_dz, dz, iy, slot, arrived):
         owner, dest = at(owner_dz, iy), at(dz, iy)
-        remote(wsend.at[owner], wrecv.at[slot], w_send, w_recv, gx, dest).start()
+        remote(wsend.at[owner], wrecv.at[slot], w_send, arrived, gx, dest).start()
 
     def send_first(dz, x):
         dest = at(dz, x)
@@ -153,39 +154,44 @@
         dest = at(dz, x)
         remote(fsend2.at[dest], frecv2.at[me], f_send2, f_recv2, gx, dest).start()
 
-    def wall_here(k, c):
+    odd = lax.rem(y, 2)
+    dz8 = NEAR - 2 * NEAR * odd
+    slot8 = jnp.where(odd == 1, LEFT, RIGHT) + 4 * GY + y // 2
+
+    def wall_8(iy, c):
+        send_wall(8, dz8, iy, slot8, s_recv)
+        return c
+
+    def wall_summed(k, c):
+        level, iy = 3 - k // GY, lax.rem(k, GY)
+        send_wall(4 + level, level, iy, RIGHT + level * GY + y, s_recv)
+        send_wall(-4 - level, -level, iy, LEFT + level * GY + y, s_recv)
+        return c
+
+    def wall_summed_here(k, c):
         iy = lax.rem(y + k, GY)
-        send_wall(0, 0, iy, DIRECT + 3 * GY + y)
-        send_wall(4, 0, iy, RIGHT + y)
-        send_wall(-4, 0, iy, LEFT + y)
-        return c
-
-    lax.fori_loop(1, GY, wall_here, 0)
+        send_wall(4, 0, iy, RIGHT + y, s_recv)
+        send_wall(-4, 0, iy, LEFT + y, s_recv)
+        return c
+
+    def wall_direct(k, c):
+        level, iy = 3 - k // GY, lax.rem(k, GY)
+        send_wall(level, level, iy, DIRECT + (3 + level) * GY + y, w_recv)
+        send_wall(-level, -level, iy, DIRECT + (3 - level) * GY + y, w_recv)
+        return c
+
+    def wall_direct_here(k, c):
+        send_wall(0, 0, lax.rem(y + k, GY), DIRECT + 3 * GY + y, w_recv)
+        return c
+
+    lax.fori_loop(0, GY, wall_8, 0)
+    lax.fori_loop(0, 3 * GY, wall_summed, 0)
+    lax.fori_loop(1, GY, wall_summed_here, 0)
+    lax.fori_loop(0, 3 * GY, wall_direct, 0)
+    lax.fori_loop(1, GY, wall_direct_here, 0)
     wrecv[DIRECT + 3 * GY + y] = wsend[me]
     wrecv[RIGHT + y] = wsend[at(4, y)]
     wrecv[LEFT + y] = wsend[at(-4, y)]
-
-    def wall_at(level):
-        def body(iy, c):
-            send_wall(level, level, iy, DIRECT + (3 + level) * GY + y)
-            send_wall(-level, -level, iy, DIRECT + (3 - level) * GY + y)
-            send_wall(4 + level, level, iy, RIGHT + level * GY + y)
-            send_wall(-4 - level, -level, iy, LEFT + level * GY + y)
-            return c
-
-        lax.fori_loop(0, GY, body, 0)
-
-    for level in (1, 2, 3):
-        wall_at(level)
-    odd = lax.rem(y, 2)
-    dz8 = NEAR - 2 * NEAR * odd
-    slot8 = jnp.where(odd == 1, LEFT, RIGHT) + 4 * GY + y // 2
-
-    def wall_8(iy, c):
-        send_wall(8, dz8, iy, slot8)
-        return c
-
-    lax.fori_loop(0, GY, wall_8, 0)
 
     def fields_at(send, first, last, xs):
         def body(level, c):
@@ -214,42 +220,50 @@
     frecv[me] = fsend[me]
     frecv2[me] = fsend2[me]
 
+    others = pl.ds(0, NGZ - 1)
+
+    def sums(first, last, groups):
+        slots = (last - first) * CAP
+        got = wrecv[first:last, CAP, :].astype(BF16)[:, 0:CAP]
+        tile = (iota((CAP, slots), 0) == lax.rem(iota((CAP, slots), 1), CAP)).astype(BF16)
+        spread = dot(got, tile)
+        mine = iota((last - first, slots), 0) == iota((last - first, slots), 1) // CAP
+        cell_row = jnp.sum(jnp.where(mine, spread, 0.0), axis=0, keepdims=True)
+        place = iota((groups * 64, slots), 0)
+        group = iota((groups * 64, slots), 1) // (slots // groups)
+        inside = (lax.rem(place, 16) < ZL) & (place // 64 == group)
+        target = jnp.where(inside, lax.rem(place, 64) // 16 * ZL + lax.rem(place, 16), -2)
+        onehot = jnp.where(target.astype(F32) == cell_row, 1.0, 0.0).astype(BF16)
+        r_hi, r_lo = split(wrecv[first:last, 0:CAP, :].reshape(slots, 128))
+        wall = dot(onehot, r_hi) + dot(onehot, r_lo)
+        return wall.reshape(groups * XL, 16, 128)[:, 0:ZL]
+
+    def send_far_sums(xc, c):
+        there = gx, at(4, xc)
+        remote(xsend.at[4 + xc], xrecv.at[4 + y], x_send, x_recv, *there).start()
+        there = gx, at(-4, xc)
+        remote(xsend.at[8 + xc], xrecv.at[8 + y], x_send, x_recv, *there).start()
+        return c
+
+    def send_near_sums(k, c):
+        xc = lax.rem(y + k, XL)
+        remote(xsend.at[xc], xrecv.at[y], x_send, x_recv, gx, at(0, xc)).start()
+        return c
+
     pl.semaphore_wait(known, 2)
     fields_at(send_first, NEAR + 1, 8, range(XL))
     for x in range(XL):
         send_first(8, x)
-    others = pl.ds(0, NGZ - 1)
-    got_wall = pl.ds(0, NGZ - 3)
-    pltpu.make_async_copy(wsend.at[got_wall], wrecv.at[got_wall], w_recv).wait()
-    slots = NGZ * CAP
-    got = wrecv[:, CAP, :].astype(BF16)[:, 0:CAP]
-    tile = (iota((CAP, slots), 0) == lax.rem(iota((CAP, slots), 1), CAP)).astype(BF16)
-    spread = dot(got, tile)
-    mine = iota((NGZ, slots), 0) == iota((NGZ, slots), 1) // CAP
-    cell_row = jnp.sum(jnp.where(mine, spread, 0.0), axis=0, keepdims=True)
-    place = iota((192, slots), 0)
-    slot = iota((192, slots), 1) // CAP
-    group = jnp.where(slot >= LEFT, 2, jnp.where(slot >= RIGHT, 1, 0))
-    inside = (lax.rem(place, 16) < ZL) & (place // 64 == group)
-    target = jnp.where(inside, lax.rem(place, 64) // 16 * ZL + lax.rem(place, 16), -2)
-    onehot = jnp.where(target.astype(F32) == cell_row, 1.0, 0.0).astype(BF16)
-    r_hi, r_lo = split(wrecv[:, 0:CAP, :].reshape(slots, 128))
-    wall = (dot(onehot, r_hi) + dot(onehot, r_lo)).reshape(3 * XL, 16, 128)
-    xsend[...] = wall[:, 0:ZL]
-
-    def send_sums(xc, c):
-        there = gx, at(4, xc)
-        remote(xsend.at[4 + xc], xrecv.at[4 + y], x_send, x_recv, *there).start()
-        there = gx, at(-4, xc)
-        remote(xsend.at[8 + xc], xrecv.at[8 + y], x_send, x_recv, *there).start()
-
-        @pl.when(xc != y)
-        def _():
-            remote(xsend.at[xc], xrecv.at[y], x_send, x_recv, gx, at(0, xc)).start()
-
-        return c
-
-    lax.fori_loop(0, XL, send_sums, 0)
+    summed = pl.ds(0, NGZ - RIGHT - 2)
+    pltpu.make_async_copy(wsend.at[summed], wrecv.at[summed], s_recv).wait()
+    xsend[XL:] = sums(RIGHT, NGZ, 2)
+    lax.fori_loop(0, XL, send_far_sums, 0)
+
+
+    direct = pl.ds(0, RIGHT - 1)
+    pltpu.make_async_copy(wsend.at[direct], wrecv.at[direct], w_recv).wait()
+    xsend[0:XL] = sums(DIRECT, RIGHT, 1)
+    lax.fori_loop(1, XL, send_near_sums, 0)
     xrecv[y] = xsend[y]
     for x in range(XL):
         send_second(8, x)
@@ -269,8 +283,7 @@
 
     eleven = pl.ds(0, 3 * XL - 1)
     pltpu.make_async_copy(xsend.at[eleven], xrecv.at[eleven], x_recv).wait()
-    sums = xrecv[0:GY] + xrecv[GY : 2 * GY] + xrecv[2 * GY :]
-    given = jnp.concatenate([sums, jnp.zeros((GY, 16 - ZL, 128), F32)], axis=1)
+    given = jnp.concatenate([xrecv[0:GY] + xrecv[GY : 2 * GY] + xrecv[2 * GY :], jnp.zeros((GY, 16 - ZL, 128), F32)], axis=1)
     wall_t = jnp.transpose(given.reshape(64, 128))
     p = iota((64, 192), 0)
     col = iota((64, 192), 1)
@@ -327,7 +340,8 @@
         c.wait()
     for k in range(2):
         pltpu.make_async_copy(halo.at[k], halo.at[k], halo_send.at[k]).wait()
-    pltpu.make_async_copy(wsend.at[got_wall], wrecv.at[got_wall], w_send).wait()
+    sent = pl.ds(0, NGZ - 3)
+    pltpu.make_async_copy(wsend.at[sent], wrecv.at[sent], w_send).wait()
     pltpu.make_async_copy(xsend.at[eleven], xrecv.at[eleven], x_send).wait()
     pltpu.make_async_copy(fsend.at[others], frecv.at[others], f_send).wait()
     pltpu.make_async_copy(bsend.at[others], brecv.at[others], b_send).wait()
@@ -390,7 +404,7 @@
             first, first, first, second, second, second,
             vmem((3 * XL, ZL, 128), F32),
             vmem((3 * GY, ZL, 128), F32),
-            dma((5,)), dma((2,)), dma((2,)), *[dma] * 12,
+            dma((5,)), dma((2,)), dma((2,)), *[dma] * 13,
             pltpu.SemaphoreType.REGULAR,
         ],
         compiler_params=pltpu.CompilerParams(

time: 63.5 us -> 63.4 us (level)
  no operation moved by 1% of the time
where the time goes in v4:
time: 63.4 us; the launch traced here: 63 us
  Pallas kernels  63 us (99%)
    pallas_call x1, Pallas kernels, on_device(): pl.pallas_call(kernel, out_shape=[jax.ShapeDtypeStruct((NGZ, r, 128), F32...  60.7 us
    pallas_call x1, Pallas kernels, on_device(): pl.pallas_call(unpack, out_shape=jax.ShapeDtypeStruct((F, XL, LEV, NZ), F...  2.31 us

profile of v4, /device:TPU:6, one launch (start us, length us, event | category | flops | bytes accessed | tf_op | source)
XLA Modules:
  0.0 63.0 jit_solution(17939392525719563623)
XLA Ops:
  0.0 60.7 %shard_map.73 = (f32[64,8,128]{2,1,0:T(8,128)}, f32[64,4,128]{2,1,0:T(4,128)}) custom-call(f32[4,4,8,768]{3,2,1,0:T(8,128)} %adj_hbm.1, f32[8]{0:T(128)} %vel_ref.1, f32[8]{0:T(128)} %shear_ref.1, f32[512,512]{1,0:T(8,128)} %m_hbm.1, f32[1,1,64,8,128]{4,3,2,1,0:T(8,128)} %rows_hbm.1, s32[1,1,8,64]{3,2,1,0:T(8,128)} %bitcast.5, s32[1,1,64]{2,1,0:T(1,128)} %counts_hbm.1), custom_call_target="tpu_custom_call" | custom-call | flops 310000000 | bytes 3000000 | tf_op jit(solution)/shard_map/pallas_call | solution.py:389
  60.7 2.3 %shard_map.74 = f32[4,4,8,768]{3,2,1,0:T(8,128)} custom-call(f32[16,4,8,128]{3,2,1,0:T(8,128)} %bitcast.3, f32[16,4,4,128]{3,2,1,0:T(4,128)} %bitcast.4), custom_call_target="tpu_custom_call" | custom-call | tf_op jit(solution)/shard_map/pallas_call | solution.py:416
